TPU v7x, 32 devices: a whole 2x2x4 slice. The times are simulated.
32 devices in a mesh: node: 16 (over z, y, x), local: 2 (over core).
Axes of the slice: x: 2, y: 2, z: 4, core: 2. Of those that a mesh axis runs over, the one named last changes fastest.
Arguments:
- grad_out: bfloat16 [2048, 6144], P('node', 'local'), may hold values from -6 to 6
- gate_prob: float32 [2048, 8], P('node'), may hold values from 0.05 to 0.5
- routes: int32 [2048, 8], P('node'), may hold values from 0 to 15, all different within a row; in each aligned block of 128 rows (0 to 127, 128 to 255, ...) at most 64 rows name the same one
- paired: int32 [8], replicated, may hold values from 0 to 1, as said below
- saved_pre: bfloat16 [16, 16, 64, 2, 1024], P('node'), may hold values from -6 to 6
- w_gate: bfloat16 [16, 6144, 1024], P('node', 'local'), may hold values from -0.078125 to 0.078125
- w_up: bfloat16 [16, 6144, 1024], P('node', 'local'), may hold values from -0.078125 to 0.078125
- w_down: bfloat16 [16, 1024, 6144], P('node', None, 'local'), may hold values from -0.1875 to 0.1875
Outputs:
- grad_in: bfloat16 [2048, 6144], P('node', 'local')
- grad_down: bfloat16 [16, 1024, 6144], P('node', None, 'local')
Inputs may be any that keep to these rules, and one draw needn't show every extreme that they name: `routes`: each token names 8 different slots. Within the 128 tokens of one block (one index of node), no slot is named by more than 64 tokens, a bound that some block reaches. Exactly half of the pairs are paired, which ones drawn from the seed.
All inputs are finite; a program needn't handle non-finite values.
Results may differ from a plain program's by a relative error of at most 0.023.
Values may be sent and summed in bfloat16 or wider, within the bound.
No kernel may reach another device: no remote copies, remote signals or barrier semaphores. Data moves between devices by JAX's collectives and lax.ppermute only.
A program may use at most 128 MiB of HBM per device.

v0:
```python
import jax
import jax.numpy as jnp
from jax import lax
from jax.sharding import PartitionSpec as P


def partner_2(block, axis, apart):
    count = lax.axis_size(axis)
    route = []
    for low in range(count):
        high = low | 1 << apart
        if high != low and high < count:
            route += [(low, high), (high, low)]
    return lax.ppermute(block, axis, route)


def swiglu_grads(dhid, pre):
    gval = pre[:, 0, :].astype(jnp.float32)
    uval = pre[:, 1, :].astype(jnp.float32)
    sigm = jax.nn.sigmoid(gval)
    dgate = (dhid * uval * sigm * (1.0 + gval * (1.0 - sigm))).astype(jnp.bfloat16)
    dup = (dhid * gval * sigm).astype(jnp.bfloat16)
    return (dgate, dup)


def activation(pre):
    gval = pre[:, 0, :].astype(jnp.float32)
    uval = pre[:, 1, :].astype(jnp.float32)
    return (gval * jax.nn.sigmoid(gval) * uval).astype(jnp.bfloat16)


def body(grad_out, gate_prob, routes, paired, saved_pre, w_gate, w_up, w_down):
    tok_rows, part_slice = grad_out.shape
    nodes = lax.axis_size("node")
    top_count = routes.shape[1]
    capacity = saved_pre.shape[2]
    hidden = saved_pre.shape[4]
    rows_per_slot = nodes * capacity
    pair_count = tok_rows * top_count
    flat_routes = routes.reshape(-1)
    onehot = (flat_routes[:, None] == jnp.arange(nodes, dtype=jnp.int32)[None, :]).astype(jnp.int32)
    before = jnp.cumsum(onehot, axis=0) - onehot
    row_rank = jnp.sum(before * onehot, axis=1)
    target = flat_routes * capacity + row_rank
    source_of = (
        jnp.full((rows_per_slot,), pair_count, jnp.int32)
        .at[target]
        .set(jnp.arange(pair_count, dtype=jnp.int32))
    )
    gated = (grad_out.astype(jnp.float32)[:, None, :] * gate_prob[:, :, None]).astype(jnp.bfloat16)
    gated = jnp.concatenate(
        [gated.reshape(pair_count, part_slice), jnp.zeros((1, part_slice), jnp.bfloat16)], axis=0
    )
    outgoing = jnp.take(gated, source_of, axis=0)
    arrived = lax.all_to_all(
        outgoing.reshape(nodes, capacity, part_slice),
        "node",
        split_axis=0,
        concat_axis=0,
        tiled=True,
    )
    token_rows = arrived.reshape(rows_per_slot, part_slice)
    partial_value = lax.dot_general(
        token_rows, w_down[0], (((1,), (1,)), ((), ())), preferred_element_type=jnp.float32
    )
    partial_value = lax.optimization_barrier(partial_value.astype(jnp.bfloat16)).astype(jnp.float32)
    saved_rows = saved_pre[0].reshape(rows_per_slot, 2, hidden)
    act = activation(saved_rows)
    dhid = lax.psum(partial_value.astype(jnp.bfloat16), "local").astype(jnp.float32)
    dgate, dup = swiglu_grads(dhid, saved_rows)
    contract = (((1,), (1,)), ((), ()))
    back = lax.dot_general(dgate, w_gate[0], contract, preferred_element_type=jnp.float32)
    back = back + lax.dot_general(dup, w_up[0], contract, preferred_element_type=jnp.float32)
    back = back.astype(jnp.bfloat16)
    own = lax.dot_general(
        act, token_rows, (((0,), (0,)), ((), ())), preferred_element_type=jnp.float32
    ).astype(jnp.bfloat16)
    homing = lax.all_to_all(
        back.reshape(nodes, capacity, part_slice), "node", split_axis=0, concat_axis=0, tiled=True
    )
    picked = jnp.take(homing.reshape(rows_per_slot, part_slice), target, axis=0)
    grad_in = jnp.sum(
        picked.reshape(tok_rows, top_count, part_slice).astype(jnp.float32), axis=1
    ).astype(jnp.bfloat16)
    top_bit = nodes.bit_length() - 2
    partner = partner_2(own, "node", top_bit)
    half = nodes // 2
    my_pair = lax.axis_index("node") % half
    flag = jnp.sum(
        paired.astype(jnp.float32)
        * (jnp.arange(half, dtype=jnp.int32) == my_pair).astype(jnp.float32)
    )
    own_f = lax.optimization_barrier(own).astype(jnp.float32)
    grad_down = (own_f + flag * partner.astype(jnp.float32)).astype(jnp.bfloat16)
    return (grad_in, grad_down[None])


def solution(mesh):
    in_specs = (
        P("node", "local"),
        P("node", None),
        P("node", None),
        P(),
        P("node", None, None, None, None),
        P("node", "local", None),
        P("node", "local", None),
        P("node", None, "local"),
    )
    out_specs = (P("node", "local"), P("node", None, "local"))
    return jax.shard_map(body, mesh=mesh, in_specs=in_specs, out_specs=out_specs, check_vma=False)
```

profile of v0, /device:TPU:8, one launch (start us, length us, event | category | flops | bytes accessed | tf_op | source)
XLA Modules:
  0.0 704.0 jit_solution(2634335624163680432)
XLA Ops:
  7.2 0.8 copy.21
  8.0 0.1 eq.34
  8.1 0.1 reshape.98
  8.2 0.7 broadcast_multiply_fusion
  8.9 4.5 reduce-window.6
  13.5 0.1 copy.23
  13.8 0.1 copy.27
  13.9 0.1 mul.78
  14.1 4.3 scatter_custom_fusion
  18.4 1.3 convert_element_type.77
  19.7 0.8 copy.28
  20.5 0.1 mul.81
  20.7 1.6 fusion
  22.3 3.1 concatenate.3
  25.4 15.8 %gather_fusion = bf16[1024,3072]{1,0:T(8,128)(2,1)} fusion(bf16[1025,3072]{1,0:T(8,128)(2,1)} %concatenate.3, s32[1024]{0:T(1024)S(1)} %fusion.45), kind=kCustom, calls=%fused_computation | custom fusion | bytes 12587008 | tf_op jit(solution)/shard_map/jit(_take)/gather | solution.py:54
  41.1 3.4 broadcast_select_fusion
  44.6 145.1 %all_to_all.10 = bf16[16,64,3072]{2,1,0:T(8,128)(2,1)S(1)} all-to-all(bf16[16,64,3072]{2,1,0:T(8,128)(2,1)S(1)} %broadcast_select_fusion), channel_id=1, replica_groups=mesh['node'=16,'local'=2] {'node'}, dimensions={0} | all-to-all | bytes 12582912 | tf_op jit(solution)/shard_map/all_to_all | solution.py:55
  189.6 2.7 copy-done
  192.3 9.8 %fusion.33 = bf16[1024,1024]{1,0:T(8,128)(2,1)} fusion(bf16[1024,3072]{1,0:T(8,128)(2,1)S(1)} %bitcast.88, bf16[1,1024,3072]{2,1,0:T(8,128)(2,1)} %param.15), kind=kOutput, calls=%fused_computation.43 | convolution fusion | flops 6443499520 | bytes 14680064 | tf_op jit(solution)/shard_map/dot_general | solution.py:63
  202.2 5.6 copy.29
  207.9 14.5 %all-reduce.3.cloned.1.call-done = bf16[1024,1024]{1,0:T(8,128)(2,1)} async-done(((bf16[1024,1024]{1,0:T(8,128)(2,1)}), bf16[1024,1024]{1,0:T(8,128)(2,1)}) %all-reduce.3.cloned.1.call-update) | async-done | bytes 2097168 | tf_op jit(solution)/shard_map/psum | solution.py:69
  222.4 13.8 %fusion.3 = f32[1024,3072]{1,0:T(8,128)} fusion(bf16[1,3072,1024]{2,1,0:T(8,128)(2,1)} %param.14, bf16[1024,1024]{1,0:T(8,128)(2,1)} %all-reduce.3.cloned.1.call-done, bf16[1024,2,1024]{2,0,1:T(8,128)(2,1)} %bitcast.90), kind=kOutput, calls=%fused_computation.10 | convolution fusion | flops 6450839552 | bytes 23068672 | tf_op jit(solution)/shard_map/dot_general | solution.py:73
  236.2 14.6 %add_convert_fusion.1 = bf16[1024,3072]{1,0:T(8,128)(2,1)} fusion(f32[1024,3072]{1,0:T(8,128)} %fusion.3, bf16[1,3072,1024]{2,1,0:T(8,128)(2,1)} %param.13, bf16[1024,1024]{1,0:T(8,128)(2,1)} %all-reduce.3.cloned.1.call-done, bf16[1024,2,1024]{2,0,1:T(8,128)(2,1)S(1)} %bitcast.92), kind=kOutput, calls=%fused_computation.6 | convolution fusion | flops 6462373888 | bytes 31457280 | tf_op jit(solution)/shard_map/dot_general | solution.py:72
  250.8 7.0 all-to-all-start.1
  257.8 12.5 %convolution_convert_fusion = bf16[1024,3072]{1,0:T(8,128)(2,1)} fusion(bf16[1024,3072]{1,0:T(8,128)(2,1)} %bitcast.89, bf16[1024,2,1024]{2,0,1:T(8,128)(2,1)} %bitcast.91), kind=kOutput, calls=%fused_computation.23 | convolution fusion | flops 6453985280 | bytes 16777216 | tf_op jit(solution)/shard_map/dot_general | solution.py:75
  270.3 2.4 collective-permute-start
  272.8 0.1 copy.26
  273.0 0.6 fusion.48
  273.6 390.1 %collective-permute-done = bf16[1024,3072]{1,0:T(8,128)(2,1)} collective-permute-done((bf16[1024,3072]{1,0:T(8,128)(2,1)}, bf16[1024,3072]{1,0:T(8,128)(2,1)}, u32[]{:S(2)}, u32[]{:S(2)}) %collective-permute-start) | collective-permute-done | bytes 6291488 | tf_op jit(solution)/shard_map/ppermute | solution.py:14
  663.7 10.9 %fusion.1 = bf16[1,1024,3072]{2,1,0:T(8,128)(2,1)} fusion(bf16[1024,3072]{1,0:T(8,128)(2,1)} %collective-permute-done, bf16[1024,3072]{1,0:T(8,128)(2,1)} %convolution_convert_fusion, f32[]{:T(128)} %fusion.48), kind=kLoop, calls=%fused_computation.7 | loop fusion | flops 15728640 | bytes 18874372 | tf_op jit(solution)/shard_map/broadcast_in_dim | solution.py:95
  674.6 15.8 %gather_fusion.1 = bf16[1024,3072]{1,0:T(8,128)(2,1)} fusion(bf16[1024,3072]{1,0:T(8,128)(2,1)} %bitcast.14, s32[1024]{0:T(1024)S(1)} %broadcast_clamp_fusion), kind=kCustom, calls=%fused_computation.1 | custom fusion | bytes 12587008 | tf_op jit(solution)/shard_map/jit(_take)/gather | solution.py:81
  690.4 6.8 fusion.2
  (26 shorter events, 0.6 us)
Async XLA Ops:
  7.2 215.2 %all-reduce.3.cloned.1.call-start = ((), (), s32[]{:S(2)}) async-start(), calls=%async_computation.2 | async-start | bytes 4194304 | tf_op jit(solution)/shard_map/psum | solution.py:69
  189.6 2.7 copy-start
  222.4 13.9 %copy-start.1 = (bf16[1,16,64,2,1024]{4,2,1,3,0:T(8,128)(2,1)S(1)}, bf16[1,16,64,2,1024]{4,2,1,3,0:T(8,128)(2,1)}, u32[]{:S(2)}) copy-start(bf16[1,16,64,2,1024]{4,2,1,3,0:T(8,128)(2,1)} %copy.29) | copy-start | bytes 12582916
  250.8 423.8 %all-to-all-start.1 = ((bf16[16,64,3072]{2,1,0:T(8,128)(2,1)}), bf16[16,64,3072]{2,1,0:T(8,128)(2,1)}, u32[]{:S(2)}, u32[]{:S(2)}) async-start(bf16[16,64,3072]{2,1,0:T(8,128)(2,1)} %bitcast.87), calls=%async_computation.1 | async-start | bytes 12582912 | tf_op jit(solution)/shard_map/all_to_all | solution.py:78
  257.8 15.0 %copy-start.2 = (s32[128,8]{0,1:T(8,128)S(1)}, s32[128,8]{0,1:T(8,128)}, u32[]{:S(2)}) copy-start(s32[128,8]{0,1:T(8,128)} %param.10) | copy-start | bytes 12292
  257.8 15.2 %copy-start.3 = (s32[8]{0:T(128)S(1)}, s32[8]{0:T(128)}, u32[]{:S(2)}) copy-start(s32[8]{0:T(128)} %param.11) | copy-start | bytes 100
  270.3 393.4 %collective-permute-start = (bf16[1024,3072]{1,0:T(8,128)(2,1)}, bf16[1024,3072]{1,0:T(8,128)(2,1)}, u32[]{:S(2)}, u32[]{:S(2)}) collective-permute-start(bf16[1024,3072]{1,0:T(8,128)(2,1)} %convolution_convert_fusion), channel_id=1, source_target_pairs={{0,16},{16,0},{2,18},{18,2},{4,20},{20,4},{6,22},{22,6},{8,24},{24... | collective-permute-start | bytes 18874376 | tf_op jit(solution)/shard_map/ppermute | solution.py:14
Sparse Core Ops, SparseCore 0:
  202.3 19.9 all-reduce.2
where the time goes:
time: 711 us; the launch traced here: 704 us
  waiting for transfers between devices  405 us (57%)
  blocking collectives  145 us (20%)
  matrix products  50.8 us (7%)
  local copies, waits for them, and re-layouts  50 us (7%)
  other arithmetic  30 us (4%)
  between operations  14.2 us (2%)
  starting transfers between devices  9.37 us (1%)
    ppermute x1, waiting for transfers between devices, partner_2(): return lax.ppermute(block, axis, route)  390 us
    all_to_all x1, blocking collectives, body(): lax.all_to_all(outgoing.reshape(nodes, capacity, part_slice), 'node', spl...  145 us
    gather x1, local copies, waits for them, and re-layouts, body(): outgoing = jnp.take(gated, source_of, axis=0)  15.8 us
    gather x1, local copies, waits for them, and re-layouts, body(): picked = jnp.take(homing.reshape(rows_per_slot, part_slice), target, axis=0)  15.8 us
    dot_general x1, matrix products, body(): lax.dot_general(dgate, w_gate[0], contract, preferred_element_type=jnp.fl...  14.6 us
    psum x1, waiting for transfers between devices, body(): lax.psum(partial_value.astype(jnp.bfloat16), 'local').astype(jnp.float32)  14.5 us
  transfers between devices with their start and end apart: 3, of which 2 were waited for; matrix products, arithmetic and copies ran while one was open for 4% of the time, Pallas kernels for 0%

commit v1 on v0

v1 whole, which is shorter than its diff:
```python
import functools

import jax
import jax.numpy as jnp
from jax import lax
from jax.experimental import pallas as pl
from jax.experimental.pallas import tpu as pltpu
from jax.sharding import PartitionSpec as P

F32 = jnp.float32
BF16 = jnp.bfloat16
LANES = 128
MIB = 1 << 20
PLANE = 4
CONTRACT_LAST = (((1,), (1,)), ((), ()))


def params(mib, ndims=0):
    sem = ("arbitrary",) * ndims if ndims else None
    return pltpu.CompilerParams(vmem_limit_bytes=mib * MIB, dimension_semantics=sem)


def cost(flops, nbytes):
    return pl.CostEstimate(flops=int(flops), bytes_accessed=int(nbytes), transcendentals=0)


def dot(a, b):
    return jnp.dot(a, b, preferred_element_type=F32)


def attach_kernel(top, grad_ref, routes_ref, gate_ref, out_ref):
    tok, feats = grad_ref.shape
    out_ref[:, :feats] = grad_ref[...]
    gate = gate_ref[...]
    high = gate.astype(BF16).astype(F32)
    mid = (gate - high).astype(BF16).astype(F32)
    low = gate - high - mid
    names = routes_ref[...].astype(F32)
    pad = jnp.zeros((tok, LANES - 4 * top), F32)
    out_ref[:, feats:] = jnp.concatenate([names, high, mid, low, pad], axis=1).astype(BF16)


def attach(grad_out, routes, gate_prob):
    tok, feats = grad_out.shape
    top = routes.shape[1]
    return pl.pallas_call(
        functools.partial(attach_kernel, top),
        out_shape=jax.ShapeDtypeStruct((tok, feats + LANES), BF16),
        compiler_params=params(16),
        name="attach",
    )(grad_out, routes, gate_prob)


def ranks(meta, slot, top, width):
    tok = meta.shape[0]
    lane = lax.broadcasted_iota(jnp.int32, meta.shape, 1)
    hit = jnp.where((lane < top) & (meta == slot.astype(F32)), 1.0, 0.0)
    named = jnp.broadcast_to(jnp.sum(hit, axis=1, keepdims=True), (tok, width))
    row = lax.broadcasted_iota(jnp.int32, (tok, tok), 0)
    col = lax.broadcasted_iota(jnp.int32, (tok, tok), 1)
    earlier = jnp.where(row > col, 1.0, 0.0).astype(BF16)
    return jnp.where(named > 0.5, dot(earlier, named.astype(BF16)), -1.0)


def row_gates(picked, slot, top):
    lane = lax.broadcasted_iota(jnp.int32, picked.shape, 1)
    high = pltpu.roll(picked, LANES - top, 1)
    mid = pltpu.roll(picked, LANES - 2 * top, 1)
    low = pltpu.roll(picked, LANES - 3 * top, 1)
    gate = (high + mid) + low
    chosen = jnp.where((lane < top) & (picked == slot.astype(F32)), gate, 0.0)
    return jnp.sum(chosen, axis=1, keepdims=True)


def selection(meta_refs, slot, top, cap, sel_ref, gate_ref):
    for q, meta_ref in enumerate(meta_refs):
        meta = meta_ref[...]
        rank = ranks(meta.astype(F32), slot, top, LANES)
        turned = jnp.transpose(rank)[:cap]
        want = lax.broadcasted_iota(jnp.int32, turned.shape, 0).astype(F32)
        sel = jnp.where(turned == want, 1.0, 0.0).astype(BF16)
        sel_ref[q * cap : (q + 1) * cap, :] = sel
        gates = row_gates(dot(sel, meta), slot, top)
        gate_ref[q * cap : (q + 1) * cap, :] = jnp.broadcast_to(gates, (cap, LANES))


def rows_kernel(top, cap, first, with_product, who_ref, *refs):
    z_ref, x_ref, y_ref, xya_ref, xyb_ref, mz_ref, mx_ref, my_ref, mxy_ref = refs[:9]
    if with_product:
        wd_ref, rows_ref, part_ref, sel_ref, gate_ref, acc_ref = refs[9:]
        slot = who_ref[0]
    else:
        rows_ref, sel_ref, gate_ref = refs[9:]
        slot = who_ref[2]
    step = pl.program_id(0)

    @pl.when(step == 0)
    def _():
        selection((mz_ref, mx_ref, my_ref, mxy_ref), slot, top, cap, sel_ref, gate_ref)
        if with_product:
            acc_ref[...] = jnp.zeros_like(acc_ref)

    def put(q, block):
        at = slice(q * cap, (q + 1) * cap)
        rows_ref[at, :] = (dot(sel_ref[at, :], block) * gate_ref[at, :1]).astype(BF16)

    put(0, z_ref[...])
    put(1, x_ref[...])
    put(2, y_ref[...])

    @pl.when(step < first)
    def _():
        put(3, xya_ref[...])

    @pl.when(step >= first)
    def _():
        put(3, xyb_ref[...])

    if with_product:
        acc_ref[...] += lax.dot_general(
            rows_ref[...], wd_ref[...], CONTRACT_LAST, preferred_element_type=F32
        )

        @pl.when(step == pl.num_programs(0) - 1)
        def _():
            part_ref[...] = acc_ref[...].astype(BF16)


def make_rows(who, blocks, w_down, sizes, name):
    tok, feats, piece_a, chunk, cap, top = sizes
    piece_b = feats - piece_a
    first = piece_a // chunk
    steps = feats // chunk
    z, x, y, xya, xyb = blocks
    by_step = pl.BlockSpec((tok, chunk), lambda i, who: (0, i))
    meta = pl.BlockSpec((tok, LANES), lambda i, who: (0, feats // LANES))
    in_specs = [by_step] * 3 + [
        pl.BlockSpec((tok, chunk), lambda i, who: (0, jnp.minimum(i, first - 1))),
        pl.BlockSpec((tok, chunk), lambda i, who: (0, jnp.maximum(i - first, 0))),
        meta,
        meta,
        meta,
        pl.BlockSpec((tok, LANES), lambda i, who: (0, piece_b // LANES)),
    ]
    args = [z, x, y, xya, xyb, z, x, y, xyb]
    count = PLANE * cap
    out_shape = [jax.ShapeDtypeStruct((count, feats), BF16)]
    out_specs = [pl.BlockSpec((count, chunk), lambda i, who: (0, i))]
    scratch = [pltpu.VMEM((count, tok), BF16), pltpu.VMEM((count, LANES), F32)]
    flops = 2 * count * tok * feats
    nbytes = 2 * feats * (PLANE * tok + count)
    if w_down is not None:
        hidden = w_down.shape[0]
        in_specs.append(pl.BlockSpec((hidden, chunk), lambda i, who: (0, i)))
        args.append(w_down)
        out_shape.append(jax.ShapeDtypeStruct((count, hidden), BF16))
        out_specs.append(pl.BlockSpec((count, hidden), lambda i, who: (0, 0)))
        scratch.append(pltpu.VMEM((count, hidden), F32))
        flops += 2 * count * feats * hidden
        nbytes += 2 * hidden * feats
    return pl.pallas_call(
        functools.partial(rows_kernel, top, cap, first, w_down is not None),
        grid_spec=pltpu.PrefetchScalarGridSpec(
            num_scalar_prefetch=1,
            grid=(steps,),
            in_specs=in_specs,
            out_specs=out_specs,
            scratch_shapes=scratch,
        ),
        out_shape=out_shape,
        compiler_params=params(24, 1),
        cost_estimate=cost(flops, nbytes),
        name=name,
    )(who, *args)


def act_kernel(cap, many, who_ref, g_ref, u_ref, out_ref):
    rows = g_ref.shape[0]
    width = many * cap
    for i in range(rows // width):
        pieces = []
        for q in range(many):
            at = pl.ds(pl.multiple_of((who_ref[0] ^ (i * many + q)) * cap, cap), cap)
            g = g_ref[at, :].astype(F32)
            pieces.append(g * jax.nn.sigmoid(g) * u_ref[at, :].astype(F32))
        block = jnp.concatenate(pieces, axis=0) if many > 1 else pieces[0]
        out_ref[:, i * width : (i + 1) * width] = jnp.transpose(block).astype(BF16)


def activations(who, g, u, cap):
    rows, hidden = g.shape
    many = max(1, LANES // cap)
    return pl.pallas_call(
        functools.partial(act_kernel, cap, many),
        in_specs=[
            pl.BlockSpec(memory_space=pltpu.SMEM),
            pl.BlockSpec(memory_space=pltpu.VMEM),
            pl.BlockSpec(memory_space=pltpu.VMEM),
        ],
        out_specs=pl.BlockSpec(memory_space=pltpu.VMEM),
        out_shape=jax.ShapeDtypeStruct((hidden, rows), BF16),
        compiler_params=params(24),
        cost_estimate=cost(20 * rows * hidden, 6 * rows * hidden),
        name="activation",
    )(who, g, u)


def back_kernel(cap, first, who_ref, po_ref, pr_ref, *refs):
    g_refs, u_refs = refs[:PLANE], refs[PLANE : 2 * PLANE]
    wg_ref, wu_ref, keep_ref, sa_ref, sb_ref, dg_ref, du_ref = refs[2 * PLANE :]
    step = pl.program_id(0)

    @pl.when(step == 0)
    def _():
        for q in range(PLANE):
            at = slice(q * cap, (q + 1) * cap)
            dhid = po_ref[at, :].astype(F32) + pr_ref[at, :].astype(F32)
            g = g_refs[q][...].astype(F32)
            u = u_refs[q][...].astype(F32)
            sig = jax.nn.sigmoid(g)
            dg_ref[at, :] = (dhid * u * sig * (1.0 + g * (1.0 - sig))).astype(BF16)
            du_ref[at, :] = (dhid * g * sig).astype(BF16)

    back = lax.dot_general(dg_ref[...], wg_ref[...], CONTRACT_LAST, preferred_element_type=F32)
    back += lax.dot_general(du_ref[...], wu_ref[...], CONTRACT_LAST, preferred_element_type=F32)
    back = back.astype(BF16)

    @pl.when(step < first)
    def _():
        keep_ref[:cap, :] = back[:cap]
        keep_ref[cap:, :] = back[2 * cap : 3 * cap]
        sa_ref[:cap, :] = back[cap : 2 * cap]
        sa_ref[cap:, :] = back[3 * cap :]

    @pl.when(step >= first)
    def _():
        keep_ref[...] = back[: 2 * cap]
        sb_ref[...] = back[2 * cap :]


def make_back(who, part_own, part_other, g, u, w_gate, w_up, sizes, group, name):
    tok, feats, piece_a, chunk, cap, top = sizes
    hidden = g.shape[1]
    first = piece_a // chunk
    count = PLANE * cap

    def saved(q):
        return pl.BlockSpec((cap, hidden), lambda i, who: (who[0] ^ (PLANE * group + q), 0))

    whole = pl.BlockSpec((count, hidden), lambda i, who: (0, 0))
    weight = pl.BlockSpec((chunk, hidden), lambda i, who: (i, 0))
    return pl.pallas_call(
        functools.partial(back_kernel, cap, first),
        grid_spec=pltpu.PrefetchScalarGridSpec(
            num_scalar_prefetch=1,
            grid=(feats // chunk,),
            in_specs=[whole, whole]
            + [saved(q) for q in range(PLANE)] * 2
            + [weight, weight],
            out_specs=[
                pl.BlockSpec((2 * cap, chunk), lambda i, who: (0, i)),
                pl.BlockSpec((2 * cap, chunk), lambda i, who: (0, jnp.minimum(i, first - 1))),
                pl.BlockSpec((2 * cap, chunk), lambda i, who: (0, jnp.maximum(i - first, 0))),
            ],
            scratch_shapes=[pltpu.VMEM((count, hidden), BF16)] * 2,
        ),
        out_shape=[
            jax.ShapeDtypeStruct((2 * cap, feats), BF16),
            jax.ShapeDtypeStruct((2 * cap, piece_a), BF16),
            jax.ShapeDtypeStruct((2 * cap, feats - piece_a), BF16),
        ],
        compiler_params=params(24, 1),
        cost_estimate=cost(4 * count * feats * hidden, 4 * feats * hidden + 2 * count * feats),
        name=name,
    )(who, part_own, part_other, *([g] * PLANE), *([u] * PLANE), w_gate, w_up)


def spread(meta, slot, other, top, cap):
    width = max(LANES, 2 * cap)
    mine = ranks(meta, slot, top, width)[:, : 2 * cap]
    theirs = ranks(meta, other, top, width)[:, : 2 * cap]
    lane = lax.broadcasted_iota(jnp.int32, mine.shape, 1)
    want = lane.astype(F32)
    off = jnp.where(lane < cap, mine, theirs + cap) - want
    return jnp.where(off == 0.0, 1.0, 0.0).astype(BF16)


def join_kernel(top, cap, piece_a, who_ref, mz, mx, my, keep, ra, rb, out_ref, sa_ref, sb_ref):
    me = who_ref[0]
    z, x, y = mz[...].astype(F32), mx[...].astype(F32), my[...].astype(F32)

    def tokens(meta, other, kept, got):
        hot = spread(meta, me, me ^ other, top, cap)
        return dot(hot, jnp.concatenate([kept, got], axis=0)).astype(BF16)

    out_ref[:, :piece_a] = tokens(z, 1, keep[:cap, :piece_a], ra[:cap, :])
    sa_ref[...] = tokens(y, 1, keep[cap:, :piece_a], ra[cap:, :])
    out_ref[:, piece_a:] = tokens(z, 2, keep[:cap, piece_a:], rb[:cap, :])
    sb_ref[...] = tokens(x, 2, keep[cap:, piece_a:], rb[cap:, :])


def join(who, z, x, y, keep, got_a, got_b, sizes, name):
    tok, feats, piece_a, chunk, cap, top = sizes
    piece_b = feats - piece_a
    meta = pl.BlockSpec((tok, LANES), lambda i, who: (0, feats // LANES))

    def full(a):
        return pl.BlockSpec(a.shape, lambda i, who: (0, 0))

    shapes = [(tok, feats), (tok, piece_a), (tok, piece_b)]
    return pl.pallas_call(
        functools.partial(join_kernel, top, cap, piece_a),
        grid_spec=pltpu.PrefetchScalarGridSpec(
            num_scalar_prefetch=1,
            grid=(1,),
            in_specs=[meta, meta, meta, full(keep), full(got_a), full(got_b)],
            out_specs=[pl.BlockSpec(s, lambda i, who: (0, 0)) for s in shapes],
        ),
        out_shape=[jax.ShapeDtypeStruct(s, BF16) for s in shapes],
        compiler_params=params(24, 1),
        cost_estimate=cost(8 * tok * cap * feats, 4 * (2 * cap + tok) * feats),
        name=name,
    )(who, z, x, y, keep, got_a, got_b)


def add_kernel(piece_a, kept, ga, gb, *refs):
    *others, out_ref = refs
    for at, got in ((slice(0, piece_a), ga), (slice(piece_a, kept.shape[1]), gb)):
        total = kept[:, at].astype(F32) + got[...].astype(F32)
        for other in others:
            total += other[:, at].astype(F32)
        out_ref[:, at] = total.astype(BF16)


def add(kept, got_a, got_b, others, name):
    return pl.pallas_call(
        functools.partial(add_kernel, got_a.shape[1]),
        out_shape=jax.ShapeDtypeStruct(kept.shape, BF16),
        compiler_params=params(24),
        cost_estimate=cost(4 * kept.size, 2 * kept.size * (3 + len(others))),
        name=name,
    )(kept, got_a, got_b, *others)


def own_kernel(groups, flag_ref, act_ref, pact_ref, *refs):
    rows, prows, out_ref = refs[:groups], refs[groups : 2 * groups], refs[-1]
    count = rows[0].shape[0]

    def product(a_ref, b_refs, order):
        total = None
        for g in range(groups):
            at = order(g) * count
            term = dot(a_ref[:, at : at + count], b_refs[g][...])
            total = term if total is None else total + term
        return total.astype(BF16).astype(F32)

    own = product(act_ref, rows, lambda g: g)
    paired = product(pact_ref, prows, lambda g: g ^ (groups // 2))
    out_ref[...] = (own + flag_ref[0] * paired).astype(BF16)


def make_own(flag, act, pact, rows, prows, before, start, count, chunk, feats, name):
    groups = len(rows)
    hidden, width = act.shape
    full = pl.BlockSpec((hidden, width), lambda i, flag: (0, 0))
    part = pl.BlockSpec((rows[0].shape[0], chunk), lambda i, flag: (0, i + start))
    in_specs = [full, full] + [part] * (2 * groups)
    args = [flag, act, pact, *rows, *prows]
    aliases = {}
    if before is not None:
        in_specs.append(pl.BlockSpec(memory_space=pl.ANY))
        aliases = {len(args): 0}
        args.append(before)
    return pl.pallas_call(
        functools.partial(own_kernel, groups),
        grid_spec=pltpu.PrefetchScalarGridSpec(
            num_scalar_prefetch=1,
            grid=(count,),
            in_specs=in_specs,
            out_specs=pl.BlockSpec((hidden, chunk), lambda i, flag: (0, i + start)),
        ),
        out_shape=jax.ShapeDtypeStruct((hidden, feats), BF16),
        input_output_aliases=aliases,
        compiler_params=params(32, 1),
        cost_estimate=cost(4 * hidden * width * chunk * count, 4 * hidden * width + 6 * width * chunk * count),
        name=name,
    )(*args)


def flip(block, bits):
    count = lax.axis_size("node")
    return lax.ppermute(block, "node", [(i, i ^ bits) for i in range(count)])


def planes(block, pairs):
    route = [(PLANE * a + i, PLANE * b + i) for a, b in pairs for i in range(PLANE)]
    return lax.ppermute(block, "node", route)


def plane_blocks(block, groups):
    if groups != 4:
        return [block] + [flip(block, PLANE * g) for g in range(1, groups)]
    plane = lax.axis_index("node") // PLANE
    middle = (plane == 1) | (plane == 2)
    inward, outward = [(1, 2), (2, 1)], [(1, 0), (2, 3)]
    one = flip(block, PLANE)
    across = planes(block, inward)
    second = planes(one, inward)
    edge_two = planes(across, outward)
    edge_three = planes(second, outward)
    return [block, one, jnp.where(middle, second, edge_two), jnp.where(middle, across, edge_three)]


def body(grad_out, gate_prob, routes, paired, saved_pre, w_gate, w_up, w_down):
    tok, feats = grad_out.shape
    nodes = lax.axis_size("node")
    locals_ = lax.axis_size("local")
    top = routes.shape[1]
    cap = saved_pre.shape[2]
    hidden = saved_pre.shape[4]
    groups = nodes // PLANE
    half = nodes // 2
    piece_a = feats // (2 * LANES) * LANES
    chunk = max(c for c in (512, 384, 256, 128) if piece_a % c == 0 and (feats - piece_a) % c == 0)
    sizes = (tok, feats, piece_a, chunk, cap, top)
    w_down, w_gate, w_up = w_down[0], w_gate[0], w_up[0]

    me = lax.axis_index("node")
    side = lax.axis_index("local")
    who = jnp.stack([me, side, me ^ half]).astype(jnp.int32)
    flag = jnp.sum(jnp.where(jnp.arange(half, dtype=jnp.int32) == me % half, paired, 0)).astype(F32)[None]

    block = attach(grad_out, routes, gate_prob)
    zs = plane_blocks(block, groups)
    xs = [flip(z, 1) for z in zs]
    ys = [flip(z, 2) for z in zs]
    xyas = [flip(x[:, :piece_a], 2) for x in xs]
    xybs = [flip(y[:, piece_a:], 1) for y in ys]

    saved_rows = saved_pre[0].reshape(nodes * cap, 2, hidden)
    g_rows, u_rows = saved_rows[:, 0, :], saved_rows[:, 1, :]
    act = activations(who, g_rows, u_rows, cap)

    share = hidden // locals_
    mine = flip(lax.dynamic_slice_in_dim(act, side * share, share, 0), half)
    ring = [(i, (i + 1) % locals_) for i in range(locals_)]
    pieces = [mine]
    for _ in range(locals_ - 1):
        pieces.append(lax.ppermute(pieces[-1], "local", ring))
    pact = jnp.zeros((hidden, nodes * cap), BF16)
    for i, piece in enumerate(pieces):
        pact = lax.dynamic_update_slice_in_dim(pact, piece, (side - i) % locals_ * share, 0)

    order = list(range(1, groups)) + [0]
    rows, prows, homing = [None] * groups, [None] * groups, []
    for g in order:
        blocks = (zs[g], xs[g], ys[g], xyas[g], xybs[g])
        rows[g], part = make_rows(who, blocks, w_down, sizes, f"partial_{g}")
        if locals_ == 2:
            other = lax.ppermute(part, "local", ring)
        else:
            other = jnp.zeros(part.shape, F32)
            piece = part
            for _ in range(locals_ - 1):
                piece = lax.ppermute(piece, "local", ring)
                other = other + piece.astype(F32)
        keep, send_a, send_b = make_back(
            who, part, other, g_rows, u_rows, w_gate, w_up, sizes, g, f"back_{g}"
        )
        got_a, got_b = flip(send_a, 1), flip(send_b, 2)
        kept, send_a, send_b = join(who, zs[g], xs[g], ys[g], keep, got_a, got_b, sizes, f"join_{g}")
        got_a, got_b = flip(send_a, 2), flip(send_b, 1)
        if g:
            homing.append(flip(add(kept, got_a, got_b, [], f"sum_{g}"), PLANE * g))
        else:
            grad_in = add(kept, got_a, got_b, homing, "sum_last")
        (prows[g],) = make_rows(who, blocks, None, sizes, f"partner_rows_{g}")

    steps = feats // chunk
    calls = min(3, steps)
    grad_down = None
    for c in range(calls):
        start, stop = steps * c // calls, steps * (c + 1) // calls
        grad_down = make_own(
            flag, act, pact, rows, prows, grad_down, start, stop - start, chunk, feats, f"own_{c}"
        )
    return (grad_in, grad_down[None])


def solution(mesh):
    in_specs = (
        P("node", "local"),
        P("node", None),
        P("node", None),
        P(),
        P("node", None, None, None, None),
        P("node", "local", None),
        P("node", "local", None),
        P("node", None, "local"),
    )
    out_specs = (P("node", "local"), P("node", None, "local"))
    return jax.shard_map(body, mesh=mesh, in_specs=in_specs, out_specs=out_specs, check_vma=False)
```

time: 711 us -> 365 us (0.51)
  waiting for transfers between devices: 405 us -> 129 us
  blocking collectives: 145 us -> 0 us
  Pallas kernels: 0 us -> 120 us
  matrix products: 50.8 us -> 0 us
  starting transfers between devices: 9.37 us -> 58.2 us
  other arithmetic: 30 us -> 4.09 us
  between operations: 14.2 us -> 2.09 us
    ppermute x1 -> x46, waiting for transfers between devices: 390 us -> 129 us  [the longest x37 99.6 us: flip(): return lax.ppermute(block, 'node', [(i, i ^ bits) for i in range(count)])]
    all_to_all x1 -> x0, blocking collectives: 145 us -> none  [body(): lax.all_to_all(outgoing.reshape(nodes, capacity, part_slice), 'node', spl...]
    pallas_call x0 -> x25, Pallas kernels: none -> 120 us  [the longest x8 59.2 us: make_rows(): pl.pallas_call(functools.partial(rows_kernel, top, cap, first, w_down is...]
    ppermute x1 -> x46, starting transfers between devices: 2.36 us -> 58.2 us  [the longest x37 45.2 us: flip(): return lax.ppermute(block, 'node', [(i, i ^ bits) for i in range(count)])]
    dot_general x4 -> x0, matrix products: 50.8 us -> none  [the longest x1 14.6 us: body(): lax.dot_general(dgate, w_gate[0], contract, preferred_element_type=jnp.fl...]
    gather x2 -> x0, local copies, waits for them, and re-layouts: 31.5 us -> none  [the longest x1 15.8 us: body(): outgoing = jnp.take(gated, source_of, axis=0)]
    unnamed x11 -> x137, local copies, waits for them, and re-layouts: 9.94 us -> 37.9 us
    psum x1 -> x0, waiting for transfers between devices: 14.5 us -> none  [body(): lax.psum(partial_value.astype(jnp.bfloat16), 'local').astype(jnp.float32)]
  transfers between devices with their start and end apart: 3 -> 46, of which waited for: 2 -> 12; matrix products, arithmetic and copies ran while one was open for 4% -> 6% of each run, Pallas kernels for 0% -> 33%
where the time goes in v1:
time: 365 us; the launch traced here: 363 us
  waiting for transfers between devices  129 us (35%)
  Pallas kernels  120 us (33%)
  starting transfers between devices  58.2 us (16%)
  local copies, waits for them, and re-layouts  49.8 us (14%)
  other arithmetic  4.09 us (1%)
    ppermute x37, waiting for transfers between devices, flip(): return lax.ppermute(block, 'node', [(i, i ^ bits) for i in range(count)])  99.6 us
    pallas_call x8, Pallas kernels, make_rows(): pl.pallas_call(functools.partial(rows_kernel, top, cap, first, w_down is...  59.2 us
    ppermute x37, starting transfers between devices, flip(): return lax.ppermute(block, 'node', [(i, i ^ bits) for i in range(count)])  45.2 us
    unnamed x137, local copies, waits for them, and re-layouts  37.9 us
    ppermute x4, waiting for transfers between devices, planes(): return lax.ppermute(block, 'node', route)  29.5 us
    pallas_call x4, Pallas kernels, make_back(): pl.pallas_call(functools.partial(back_kernel, cap, first), grid_spec=pltp...  27.6 us
    pallas_call x3, Pallas kernels, make_own(): pl.pallas_call(functools.partial(own_kernel, groups), grid_spec=pltpu.Pre...  18.6 us
    ppermute x4, starting transfers between devices, planes(): return lax.ppermute(block, 'node', route)  12.1 us
  transfers between devices with their start and end apart: 46, of which 12 were waited for; matrix products, arithmetic and copies ran while one was open for 6% of the time, Pallas kernels for 33%

profile of v1, /device:TPU:8, one launch (start us, length us, event | category | flops | bytes accessed | tf_op | source)
XLA Modules:
  0.0 363.5 jit_solution(3696869143614368699)
XLA Ops:
  3.5 5.0 %collective-permute-start.21 = (bf16[128,3200]{1,0:T(8,128)(2,1)S(1)}, bf16[128,3200]{1,0:T(8,128)(2,1)}, u32[]{:S(2)}, u32[]{:S(2)}) collective-permute-start(bf16[128,3200]{1,0:T(8,128)(2,1)S(1)} %attach.1.refs_0_.refs_5_.mz), channel_id=1, source_target_pairs={{8,16},{10,18},{12,20},{14,22},{16,8},{18,10},{20,12},{22,14},{9,1... | collective-permute-start | bytes 2457608 | tf_op jit(solution)/shard_map/ppermute | solution.py:397
  10.1 13.5 %collective-permute-done.9.refs_0_.refs_5_.mz = bf16[128,3200]{1,0:T(8,128)(2,1)} collective-permute-done((bf16[128,3200]{1,0:T(8,128)(2,1)S(1)}, bf16[128,3200]{1,0:T(8,128)(2,1)}, u32[]{:S(2)}, u32[]{:S(2)}) %collective-permute-start.9) | collective-permute-done | bytes 819232 | tf_op jit(solution)/shard_map/ppermute | solution.py:392
  25.1 3.5 collective-permute-start.20
  30.8 5.6 %copy.14 = bf16[1,16,64,2,1024]{4,2,1,3,0:T(8,128)(2,1)} copy(bf16[1,16,64,2,1024]{4,3,2,1,0:T(2,128)(2,1)} %param.12) | data formatting | bytes 8388608 | tf_op args[4]
  48.3 22.4 %collective-permute-done.20 = bf16[128,3200]{1,0:T(8,128)(2,1)} collective-permute-done((bf16[128,3200]{1,0:T(8,128)(2,1)}, bf16[128,3200]{1,0:T(8,128)(2,1)}, u32[]{:S(2)}, u32[]{:S(2)}) %collective-permute-start.20) | collective-permute-done | bytes 819232 | tf_op jit(solution)/shard_map/ppermute | solution.py:397
  74.8 14.1 %collective-permute-done.11.refs_2_.refs_7_.my = bf16[128,3200]{1,0:T(8,128)(2,1)S(1)} collective-permute-done((bf16[128,3200]{1,0:T(8,128)(2,1)}, bf16[128,3200]{1,0:T(8,128)(2,1)S(1)}, u32[]{:S(2)}, u32[]{:S(2)}) %collective-permute-start.11) | collective-permute-done | bytes 819232 | tf_op jit(solution)/shard_map/ppermute | solution.py:392
  91.7 7.1 %collective-permute-done.33 = bf16[128,3200]{1,0:T(8,128)(2,1)S(1)} collective-permute-done((bf16[128,3200]{1,0:T(8,128)(2,1)}, bf16[128,3200]{1,0:T(8,128)(2,1)S(1)}, u32[]{:S(2)}, u32[]{:S(2)}) %collective-permute-start.33) | collective-permute-done | bytes 819232 | tf_op jit(solution)/shard_map/ppermute | solution.py:397
  103.0 7.1 %collective-permute-done.23.refs_1_.refs_6_.mx = bf16[128,3200]{1,0:T(8,128)(2,1)S(1)} collective-permute-done((bf16[128,3200]{1,0:T(8,128)(2,1)S(1)}, bf16[128,3200]{1,0:T(8,128)(2,1)S(1)}, u32[]{:S(2)}, u32[]{:S(2)}) %collective-permute-start.23) | collective-permute-done | bytes 819232 | tf_op jit(solution)/shard_map/ppermute | solution.py:392
  113.8 4.8 %collective-permute-done.12.refs_3_ = bf16[128,1536]{1,0:T(8,128)(2,1)S(1)} collective-permute-done((bf16[128,1536]{1,0:T(8,128)(2,1)S(1)}, bf16[128,1536]{1,0:T(8,128)(2,1)S(1)}, u32[]{:S(2)}, u32[]{:S(2)}) %collective-permute-start.12) | collective-permute-done | bytes 393248 | tf_op jit(solution)/shard_map/ppermute | solution.py:392
  125.0 9.2 %partial_1.1 = (bf16[256,3072]{1,0:T(8,128)(2,1)S(1)}, bf16[256,1024]{1,0:T(8,128)(2,1)}) custom-call(s32[3]{0:T(128)S(1)} %pad_add_fusion.who_ref, bf16[128,3200]{1,0:T(8,128)(2,1)} %collective-permute-done.9.refs_0_.refs_5_.mz, bf16[128,3200]{1,0:T(8,128)(2,1)} %collective-permute-done.10.refs_1_.refs_6_.mx, ...), custom_call_target="tpu_custom_call" | custom-call | flops 1811939328 | bytes 11010048 | tf_op jit(solution)/shard_map/partial_1/pallas_call | solution.py:161
  135.4 7.4 %collective-permute-done.3.refs_4_.refs_8_ = bf16[128,1664]{1,0:T(8,128)(2,1)S(1)} collective-permute-done((bf16[128,1664]{1,0:T(8,128)(2,1)S(1)}, bf16[128,1664]{1,0:T(8,128)(2,1)S(1)}, u32[]{:S(2)}, u32[]{:S(2)}) %collective-permute-start.3) | collective-permute-done | bytes 426016 | tf_op jit(solution)/shard_map/ppermute | solution.py:392
  149.5 8.4 %partial_0.1 = (bf16[256,3072]{1,0:T(8,128)(2,1)S(1)}, bf16[256,1024]{1,0:T(8,128)(2,1)S(1)}) custom-call(s32[3]{0:T(128)S(1)} %pad_add_fusion.who_ref, bf16[128,3200]{1,0:T(8,128)(2,1)S(1)} %attach.1.refs_0_.refs_5_.mz, bf16[128,3200]{1,0:T(8,128)(2,1)} %collective-permute-done.refs_1_.refs_6_.mx, bf16[128,3200]{1,0:T(8,128)(2,1)S(1)} %copy-done.14, ...), custom_call_target="tpu_custom_call" | custom-call | flops 1811939328 | bytes 11010048 | tf_op jit(solution)/shard_map/partial_0/pallas_call | solution.py:161
  166.2 8.5 %partial_2.1 = (bf16[256,3072]{1,0:T(8,128)(2,1)S(1)}, bf16[256,1024]{1,0:T(8,128)(2,1)S(1)}) custom-call(s32[3]{0:T(128)S(1)} %pad_add_fusion.who_ref, bf16[128,3200]{1,0:T(8,128)(2,1)S(1)} %copy-done.11, bf16[128,3200]{1,0:T(8,128)(2,1)S(1)} %copy-done.23, bf16[128,3200]{1,0:T(8,128)(2,1)S(1)} %copy-done.17, ...), custom_call_target="tpu_custom_call" | custom-call | flops 1811939328 | bytes 11010048 | tf_op jit(solution)/shard_map/partial_2/pallas_call | solution.py:161
  181.9 7.4 %back_1.1 = (bf16[128,3072]{1,0:T(8,128)(2,1)S(1)}, bf16[128,1536]{1,0:T(8,128)(2,1)S(1)}, bf16[128,1536]{1,0:T(8,128)(2,1)S(1)}) custom-call(s32[3]{0:T(128)S(1)} %pad_add_fusion.who_ref, bf16[256,1024]{1,0:T(8,128)(2,1)} %get-tuple-element.41.po_ref, bf16[256,1024]{1,0:T(8,128)(2,1)} %collective-permute-done.14.pr_ref, bf16[1024,1024]{1,0:T(8,128)(2,1)S(1)} %copy-done.1, ...), custom_call_target="tpu_custom_call" | custom-call | flops 3221225472 | bytes 14155776 | tf_op jit(solution)/shard_map/back_1/pallas_call | solution.py:252
  191.5 8.9 %partial_3.1 = (bf16[256,3072]{1,0:T(8,128)(2,1)S(1)}, bf16[256,1024]{1,0:T(8,128)(2,1)S(1)}) custom-call(s32[3]{0:T(128)S(1)} %pad_add_fusion.who_ref, bf16[128,3200]{1,0:T(8,128)(2,1)} %broadcast_select_fusion.refs_0_.refs_5_.mz, bf16[128,3200]{1,0:T(8,128)(2,1)} %collective-permute-done.34.refs_1_.refs_6_.mx, ...), custom_call_target="tpu_custom_call" | custom-call | flops 1811939328 | bytes 11010048 | tf_op jit(solution)/shard_map/partial_3/pallas_call | solution.py:161
  200.5 3.2 copy-done.7
  203.8 6.1 %back_0.1 = (bf16[128,3072]{1,0:T(8,128)(2,1)S(1)}, bf16[128,1536]{1,0:T(8,128)(2,1)S(1)}, bf16[128,1536]{1,0:T(8,128)(2,1)S(1)}) custom-call(s32[3]{0:T(128)S(1)} %pad_add_fusion.who_ref, bf16[256,1024]{1,0:T(8,128)(2,1)S(1)} %get-tuple-element.34.po_ref, bf16[256,1024]{1,0:T(8,128)(2,1)S(1)} %collective-permute-done.4.pr_ref, ...), custom_call_target="tpu_custom_call" | custom-call | flops 3221225472 | bytes 14155776 | tf_op jit(solution)/shard_map/back_0/pallas_call | solution.py:252
  211.3 3.3 join_1.1
  215.9 6.9 %back_2.1 = (bf16[128,3072]{1,0:T(8,128)(2,1)S(1)}, bf16[128,1536]{1,0:T(8,128)(2,1)}, bf16[128,1536]{1,0:T(8,128)(2,1)}) custom-call(s32[3]{0:T(128)S(1)} %pad_add_fusion.who_ref, bf16[256,1024]{1,0:T(8,128)(2,1)S(1)} %get-tuple-element.48.po_ref, bf16[256,1024]{1,0:T(8,128)(2,1)S(1)} %collective-permute-done.27.pr_ref, bf16[1024,1024]{1,0:T(8,128)(2,1)S(1)} %copy-done.1, ...), custom_call_target="tpu_custom_call" | custom-call | flops 3221225472 | bytes 14155776 | tf_op jit(solution)/shard_map/back_2/pallas_call | solution.py:252
  225.1 7.1 %back_3.1 = (bf16[128,3072]{1,0:T(8,128)(2,1)S(1)}, bf16[128,1536]{1,0:T(8,128)(2,1)}, bf16[128,1536]{1,0:T(8,128)(2,1)}) custom-call(s32[3]{0:T(128)S(1)} %pad_add_fusion.who_ref, bf16[256,1024]{1,0:T(8,128)(2,1)S(1)} %get-tuple-element.55.po_ref, bf16[256,1024]{1,0:T(8,128)(2,1)S(1)} %collective-permute-done.38.pr_ref, bf16[1024,1024]{1,0:T(8,128)(2,1)S(1)} %copy-done.1, ...), custom_call_target="tpu_custom_call" | custom-call | flops 3221225472 | bytes 14155776 | tf_op jit(solution)/shard_map/back_3/pallas_call | solution.py:252
  242.5 5.9 %partner_rows_0.1.refs_4_ = bf16[256,3072]{1,0:T(8,128)(2,1)S(1)} custom-call(s32[3]{0:T(128)S(1)} %pad_add_fusion.who_ref, bf16[128,3200]{1,0:T(8,128)(2,1)S(1)} %attach.1.refs_0_.refs_5_.mz, bf16[128,3200]{1,0:T(8,128)(2,1)} %collective-permute-done.refs_1_.refs_6_.mx, bf16[128,3200]{1,0:T(8,128)(2,1)S(1)} %copy-done.15, bf16[128,1536]{1,0:T(8,128)(2,1)S(1)} %copy-done.40, ...), custom_call_target="tpu_custom_call" | custom-call | flops 201326592 | bytes 4718592 | tf_op jit(solution)/shard_map/partner_rows_0/pallas_call | solution.py:161
  248.4 5.9 %partner_rows_1.1.refs_5_ = bf16[256,3072]{1,0:T(8,128)(2,1)S(1)} custom-call(s32[3]{0:T(128)S(1)} %pad_add_fusion.who_ref, bf16[128,3200]{1,0:T(8,128)(2,1)} %collective-permute-done.9.refs_0_.refs_5_.mz, bf16[128,3200]{1,0:T(8,128)(2,1)} %collective-permute-done.10.refs_1_.refs_6_.mx, bf16[128,3200]{1,0:T(8,128)(2,1)S(1)} %copy-done.21, ...), custom_call_target="tpu_custom_call" | custom-call | flops 201326592 | bytes 4718592 | tf_op jit(solution)/shard_map/partner_rows_1/pallas_call | solution.py:161
  258.3 6.2 %partner_rows_2.1.refs_6_ = bf16[256,3072]{1,0:T(8,128)(2,1)S(1)} custom-call(s32[3]{0:T(128)S(1)} %pad_add_fusion.who_ref, bf16[128,3200]{1,0:T(8,128)(2,1)S(1)} %copy-done.12, bf16[128,3200]{1,0:T(8,128)(2,1)S(1)} %copy-done.24, bf16[128,3200]{1,0:T(8,128)(2,1)S(1)} %copy-done.18, bf16[128,1536]{1,0:T(8,128)(2,1)} %collective-permute-done.25.refs_3_, ...), custom_call_target="tpu_custom_call" | custom-call | flops 201326592 | bytes 4718592 | tf_op jit(solution)/shard_map/partner_rows_2/pallas_call | solution.py:161
  266.6 6.2 %partner_rows_3.1.refs_7_ = bf16[256,3072]{1,0:T(8,128)(2,1)S(1)} custom-call(s32[3]{0:T(128)S(1)} %pad_add_fusion.who_ref, bf16[128,3200]{1,0:T(8,128)(2,1)} %broadcast_select_fusion.refs_0_.refs_5_.mz, bf16[128,3200]{1,0:T(8,128)(2,1)} %collective-permute-done.34.refs_1_.refs_6_.mx, bf16[128,3200]{1,0:T(8,128)(2,1)} %collective-permute-done.35.refs_2_.refs_7_.my, ...), custom_call_target="tpu_custom_call" | custom-call | flops 201326592 | bytes 4718592 | tf_op jit(solution)/shard_map/partner_rows_3/pallas_call | solution.py:161
  281.4 6.2 %own_0.1.refs_8_ = bf16[1024,3072]{1,0:T(8,128)(2,1)} custom-call(f32[1]{0:T(128)} %bitcast.9.flag_ref, bf16[1024,1024]{1,0:T(8,128)(2,1)S(1)} %copy-done.9, bf16[1024,1024]{1,0:T(8,128)(2,1)S(1)} %constant_dynamic-update-slice_fusion.pact_ref, bf16[256,3072]{1,0:T(8,128)(2,1)S(1)} %copy-done.28, bf16[256,3072]{1,0:T(8,128)(2,1)S(1)} %copy-done.26, ...), custom_call_target="tpu_custom_call" | custom-call | flops 4294967296 | bytes 10485760 | tf_op jit(solution)/shard_map/own_0/pallas_call | solution.py:374
  288.2 4.3 %collective-permute-start.19 = (bf16[128,3072]{1,0:T(8,128)(2,1)S(1)}, bf16[128,3072]{1,0:T(8,128)(2,1)S(1)}, u32[]{:S(2)}, u32[]{:S(2)}) collective-permute-start(bf16[128,3072]{1,0:T(8,128)(2,1)S(1)} %sum_1.1), channel_id=1, source_target_pairs={{0,8},{2,10},{4,12},{6,14},{8,0},{10,2},{12,4},{14,6},{16,24},{18,... | collective-permute-start | bytes 2359304 | tf_op jit(solution)/shard_map/ppermute | solution.py:392
  292.7 2.9 collective-permute-start.32
  298.5 6.2 %own_1.1.refs_8_ = bf16[1024,3072]{1,0:T(8,128)(2,1)} custom-call(f32[1]{0:T(128)} %bitcast.9.flag_ref, bf16[1024,1024]{1,0:T(8,128)(2,1)S(1)} %copy-done.9, bf16[1024,1024]{1,0:T(8,128)(2,1)S(1)} %constant_dynamic-update-slice_fusion.pact_ref, bf16[256,3072]{1,0:T(8,128)(2,1)S(1)} %copy-done.28, ...), custom_call_target="tpu_custom_call", output_to_operand_aliasing={{}: (11, {})} | custom-call | flops 4294967296 | bytes 10485760 | tf_op jit(solution)/shard_map/own_1/pallas_call | solution.py:374
  304.7 6.2 %own_2.1 = bf16[1024,3072]{1,0:T(8,128)(2,1)} custom-call(f32[1]{0:T(128)} %bitcast.9.flag_ref, bf16[1024,1024]{1,0:T(8,128)(2,1)S(1)} %copy-done.9, bf16[1024,1024]{1,0:T(8,128)(2,1)S(1)} %constant_dynamic-update-slice_fusion.pact_ref, bf16[256,3072]{1,0:T(8,128)(2,1)S(1)} %copy-done.28, ...), custom_call_target="tpu_custom_call", output_to_operand_aliasing={{}: (11, {})} | custom-call | flops 4294967296 | bytes 10485760 | tf_op jit(solution)/shard_map/own_2/pallas_call | solution.py:374
  310.9 6.3 %collective-permute-done.19.refs_0_ = bf16[128,3072]{1,0:T(8,128)(2,1)S(1)} collective-permute-done((bf16[128,3072]{1,0:T(8,128)(2,1)S(1)}, bf16[128,3072]{1,0:T(8,128)(2,1)S(1)}, u32[]{:S(2)}, u32[]{:S(2)}) %collective-permute-start.19) | collective-permute-done | bytes 786464 | tf_op jit(solution)/shard_map/ppermute | solution.py:392
  317.2 30.2 %collective-permute-done.32.refs_1_ = bf16[128,3072]{1,0:T(8,128)(2,1)S(1)} collective-permute-done((bf16[128,3072]{1,0:T(8,128)(2,1)S(1)}, bf16[128,3072]{1,0:T(8,128)(2,1)S(1)}, u32[]{:S(2)}, u32[]{:S(2)}) %collective-permute-start.32) | collective-permute-done | bytes 786464 | tf_op jit(solution)/shard_map/ppermute | solution.py:392
  347.4 14.8 %collective-permute-done.43.refs_2_ = bf16[128,3072]{1,0:T(8,128)(2,1)S(1)} collective-permute-done((bf16[128,3072]{1,0:T(8,128)(2,1)S(1)}, bf16[128,3072]{1,0:T(8,128)(2,1)S(1)}, u32[]{:S(2)}, u32[]{:S(2)}) %collective-permute-start.43) | collective-permute-done | bytes 786464 | tf_op jit(solution)/shard_map/ppermute | solution.py:392
  (241 shorter events, 100.6 us)
Async XLA Ops:
  3.5 25.1 %collective-permute-start.21 = (bf16[128,3200]{1,0:T(8,128)(2,1)S(1)}, bf16[128,3200]{1,0:T(8,128)(2,1)}, u32[]{:S(2)}, u32[]{:S(2)}) collective-permute-start(bf16[128,3200]{1,0:T(8,128)(2,1)S(1)} %attach.1.refs_0_.refs_5_.mz), channel_id=1, source_target_pairs={{8,16},{10,18},{12,20},{14,22},{16,8},{18,10},{20,12},{22,14},{9,1... | collective-permute-start | bytes 2457608 | tf_op jit(solution)/shard_map/ppermute | solution.py:397
  8.6 34.0 %collective-permute-start = (bf16[128,3200]{1,0:T(8,128)(2,1)S(1)}, bf16[128,3200]{1,0:T(8,128)(2,1)}, u32[]{:S(2)}, u32[]{:S(2)}) collective-permute-start(bf16[128,3200]{1,0:T(8,128)(2,1)S(1)} %attach.1.refs_0_.refs_5_.mz), channel_id=1, source_target_pairs={{0,2},{2,0},{4,6},{6,4},{8,10},{10,8},{12,14},{14,12},{16,18},{18,... | collective-permute-start | bytes 2457608 | tf_op jit(solution)/shard_map/ppermute | solution.py:392
  25.1 45.6 %collective-permute-start.20 = (bf16[128,3200]{1,0:T(8,128)(2,1)}, bf16[128,3200]{1,0:T(8,128)(2,1)}, u32[]{:S(2)}, u32[]{:S(2)}) collective-permute-start(bf16[128,3200]{1,0:T(8,128)(2,1)} %collective-permute-done.9.refs_0_.refs_5_.mz), channel_id=1, source_target_pairs={{8,16},{10,18},{12,20},{14,22},{16,8},{18,10},{20,12},{22,14},{9,1... | collective-permute-start | bytes 2457608 | tf_op jit(solution)/shard_map/ppermute | solution.py:397
  28.6 43.6 %collective-permute-start.22 = (bf16[128,3200]{1,0:T(8,128)(2,1)}, bf16[128,3200]{1,0:T(8,128)(2,1)}, u32[]{:S(2)}, u32[]{:S(2)}) collective-permute-start(bf16[128,3200]{1,0:T(8,128)(2,1)} %collective-permute-done.21), channel_id=1, source_target_pairs={{8,0},{10,2},{12,4},{14,6},{16,24},{18,26},{20,28},{22,30},{9,1},{... | collective-permute-start | bytes 2457608 | tf_op jit(solution)/shard_map/ppermute | solution.py:397
  42.6 48.0 %collective-permute-start.44 = (bf16[512,1024]{1,0:T(8,128)(2,1)}, bf16[512,1024]{1,0:T(8,128)(2,1)}, u32[]{:S(2)}, u32[]{:S(2)}) collective-permute-start(bf16[512,1024]{1,0:T(8,128)(2,1)} %constant_dynamic-slice_fusion), channel_id=1, source_target_pairs={{0,16},{2,18},{4,20},{6,22},{8,24},{10,26},{12,28},{14,30},{16,0},... | collective-permute-start | bytes 3145736 | tf_op jit(solution)/shard_map/ppermute | solution.py:392
  42.6 46.4 %collective-permute-start.1 = (bf16[128,3200]{1,0:T(8,128)(2,1)S(1)}, bf16[128,3200]{1,0:T(8,128)(2,1)S(1)}, u32[]{:S(2)}, u32[]{:S(2)}) collective-permute-start(bf16[128,3200]{1,0:T(8,128)(2,1)S(1)} %attach.1.refs_0_.refs_5_.mz), channel_id=1, source_target_pairs={{0,4},{2,6},{4,0},{6,2},{8,12},{10,14},{12,8},{14,10},{16,20},{18,... | collective-permute-start | bytes 2457608 | tf_op jit(solution)/shard_map/ppermute | solution.py:392
  45.7 55.8 %collective-permute-start.2 = (bf16[128,1536]{1,0:T(8,128)(2,1)S(1)}, bf16[128,1536]{1,0:T(8,128)(2,1)S(1)}, u32[]{:S(2)}, u32[]{:S(2)}) collective-permute-start(bf16[128,1536]{1,0:T(8,128)(2,1)S(1)} %slice.40), channel_id=1, source_target_pairs={{0,4},{2,6},{4,0},{6,2},{8,12},{10,14},{12,8},{14,10},{16,20},{18,... | collective-permute-start | bytes 1179656 | tf_op jit(solution)/shard_map/ppermute | solution.py:392
  72.2 26.6 %collective-permute-start.33 = (bf16[128,3200]{1,0:T(8,128)(2,1)}, bf16[128,3200]{1,0:T(8,128)(2,1)S(1)}, u32[]{:S(2)}, u32[]{:S(2)}) collective-permute-start(bf16[128,3200]{1,0:T(8,128)(2,1)} %collective-permute-done.20), channel_id=1, source_target_pairs={{8,0},{10,2},{12,4},{14,6},{16,24},{18,26},{20,28},{22,30},{9,1},{... | collective-permute-start | bytes 2457608 | tf_op jit(solution)/shard_map/ppermute | solution.py:397
  90.6 28.1 %collective-permute-start.12 = (bf16[128,1536]{1,0:T(8,128)(2,1)S(1)}, bf16[128,1536]{1,0:T(8,128)(2,1)S(1)}, u32[]{:S(2)}, u32[]{:S(2)}) collective-permute-start(bf16[128,1536]{1,0:T(8,128)(2,1)S(1)} %slice.44), channel_id=1, source_target_pairs={{0,4},{2,6},{4,0},{6,2},{8,12},{10,14},{12,8},{14,10},{16,20},{18,... | collective-permute-start | bytes 1179656 | tf_op jit(solution)/shard_map/ppermute | solution.py:392
  101.5 56.4 %collective-permute-start.34 = (bf16[128,3200]{1,0:T(8,128)(2,1)}, bf16[128,3200]{1,0:T(8,128)(2,1)}, u32[]{:S(2)}, u32[]{:S(2)}) collective-permute-start(bf16[128,3200]{1,0:T(8,128)(2,1)} %broadcast_select_fusion.refs_0_.refs_5_.mz), channel_id=1, source_target_pairs={{0,2},{2,0},{4,6},{6,4},{8,10},{10,8},{12,14},{14,12},{16,18},{18,... | collective-permute-start | bytes 2457608 | tf_op jit(solution)/shard_map/ppermute | solution.py:392
  110.1 49.8 %collective-permute-start.35 = (bf16[128,3200]{1,0:T(8,128)(2,1)}, bf16[128,3200]{1,0:T(8,128)(2,1)}, u32[]{:S(2)}, u32[]{:S(2)}) collective-permute-start(bf16[128,3200]{1,0:T(8,128)(2,1)} %broadcast_select_fusion.refs_0_.refs_5_.mz), channel_id=1, source_target_pairs={{0,4},{2,6},{4,0},{6,2},{8,12},{10,14},{12,8},{14,10},{16,20},{18,... | collective-permute-start | bytes 2457608 | tf_op jit(solution)/shard_map/ppermute | solution.py:392
  111.7 31.1 %collective-permute-start.3 = (bf16[128,1664]{1,0:T(8,128)(2,1)S(1)}, bf16[128,1664]{1,0:T(8,128)(2,1)S(1)}, u32[]{:S(2)}, u32[]{:S(2)}) collective-permute-start(bf16[128,1664]{1,0:T(8,128)(2,1)S(1)} %slice.41), channel_id=1, source_target_pairs={{0,2},{2,0},{4,6},{6,4},{8,10},{10,8},{12,14},{14,12},{16,18},{18,... | collective-permute-start | bytes 1277960 | tf_op jit(solution)/shard_map/ppermute | solution.py:392
  118.7 42.6 %collective-permute-start.25 = (bf16[128,1536]{1,0:T(8,128)(2,1)}, bf16[128,1536]{1,0:T(8,128)(2,1)}, u32[]{:S(2)}, u32[]{:S(2)}) collective-permute-start(bf16[128,1536]{1,0:T(8,128)(2,1)} %slice.46), channel_id=1, source_target_pairs={{0,4},{2,6},{4,0},{6,2},{8,12},{10,14},{12,8},{14,10},{16,20},{18,... | collective-permute-start | bytes 1179656 | tf_op jit(solution)/shard_map/ppermute | solution.py:392
  120.2 42.7 %collective-permute-start.26 = (bf16[128,1664]{1,0:T(8,128)(2,1)}, bf16[128,1664]{1,0:T(8,128)(2,1)}, u32[]{:S(2)}, u32[]{:S(2)}) collective-permute-start(bf16[128,1664]{1,0:T(8,128)(2,1)} %slice.47), channel_id=1, source_target_pairs={{0,2},{2,0},{4,6},{6,4},{8,10},{10,8},{12,14},{14,12},{16,18},{18,... | collective-permute-start | bytes 1277960 | tf_op jit(solution)/shard_map/ppermute | solution.py:392
  143.5 32.5 %collective-permute-start.14 = (bf16[256,1024]{1,0:T(8,128)(2,1)}, bf16[256,1024]{1,0:T(8,128)(2,1)}, u32[]{:S(2)}, u32[]{:S(2)}) collective-permute-start(bf16[256,1024]{1,0:T(8,128)(2,1)} %get-tuple-element.41.po_ref), channel_id=1, source_target_pairs={{0,1},{1,0},{2,3},{3,2},{4,5},{5,4},{6,7},{7,6},{8,9},{9,8},{10,11... | collective-permute-start | bytes 1572872 | tf_op jit(solution)/shard_map/ppermute | solution.py:460
  157.9 75.2 %collective-permute-start.45 = (bf16[512,1024]{1,0:T(8,128)(2,1)}, bf16[512,1024]{1,0:T(8,128)(2,1)S(1)}, u32[]{:S(2)}, u32[]{:S(2)}) collective-permute-start(bf16[512,1024]{1,0:T(8,128)(2,1)} %collective-permute-done.44), channel_id=1, source_target_pairs={{0,1},{1,0},{2,3},{3,2},{4,5},{5,4},{6,7},{7,6},{8,9},{9,8},{10,11... | collective-permute-start | bytes 3145736 | tf_op jit(solution)/shard_map/ppermute | solution.py:449
  160.0 40.5 %collective-permute-start.4 = (bf16[256,1024]{1,0:T(8,128)(2,1)S(1)}, bf16[256,1024]{1,0:T(8,128)(2,1)S(1)}, u32[]{:S(2)}, u32[]{:S(2)}) collective-permute-start(bf16[256,1024]{1,0:T(8,128)(2,1)S(1)} %get-tuple-element.34.po_ref), channel_id=1, source_target_pairs={{0,1},{1,0},{2,3},{3,2},{4,5},{5,4},{6,7},{7,6},{8,9},{9,8},{10,11... | collective-permute-start | bytes 1572872 | tf_op jit(solution)/shard_map/ppermute | solution.py:460
  161.3 28.0 %collective-permute-start.36 = (bf16[128,1536]{1,0:T(8,128)(2,1)S(1)}, bf16[128,1536]{1,0:T(8,128)(2,1)S(1)}, u32[]{:S(2)}, u32[]{:S(2)}) collective-permute-start(bf16[128,1536]{1,0:T(8,128)(2,1)S(1)} %slice.48), channel_id=1, source_target_pairs={{0,4},{2,6},{4,0},{6,2},{8,12},{10,14},{12,8},{14,10},{16,20},{18,... | collective-permute-start | bytes 1179656 | tf_op jit(solution)/shard_map/ppermute | solution.py:392
  162.9 28.0 %collective-permute-start.37 = (bf16[128,1664]{1,0:T(8,128)(2,1)S(1)}, bf16[128,1664]{1,0:T(8,128)(2,1)S(1)}, u32[]{:S(2)}, u32[]{:S(2)}) collective-permute-start(bf16[128,1664]{1,0:T(8,128)(2,1)S(1)} %slice.49), channel_id=1, source_target_pairs={{0,2},{2,0},{4,6},{6,4},{8,10},{10,8},{12,14},{14,12},{16,18},{18,... | collective-permute-start | bytes 1277960 | tf_op jit(solution)/shard_map/ppermute | solution.py:392
  176.0 38.6 %collective-permute-start.27 = (bf16[256,1024]{1,0:T(8,128)(2,1)S(1)}, bf16[256,1024]{1,0:T(8,128)(2,1)S(1)}, u32[]{:S(2)}, u32[]{:S(2)}) collective-permute-start(bf16[256,1024]{1,0:T(8,128)(2,1)S(1)} %get-tuple-element.48.po_ref), channel_id=1, source_target_pairs={{0,1},{1,0},{2,3},{3,2},{4,5},{5,4},{6,7},{7,6},{8,9},{9,8},{10,11... | collective-permute-start | bytes 1572872 | tf_op jit(solution)/shard_map/ppermute | solution.py:460
  209.9 23.7 %collective-permute-start.5 = (bf16[128,1536]{1,0:T(8,128)(2,1)S(1)}, bf16[128,1536]{1,0:T(8,128)(2,1)S(1)}, u32[]{:S(2)}, u32[]{:S(2)}) collective-permute-start(bf16[128,1536]{1,0:T(8,128)(2,1)S(1)} %get-tuple-element.36), channel_id=1, source_target_pairs={{0,2},{2,0},{4,6},{6,4},{8,10},{10,8},{12,14},{14,12},{16,18},{18,... | collective-permute-start | bytes 1179656 | tf_op jit(solution)/shard_map/ppermute | solution.py:392
  210.5 24.6 %collective-permute-start.6 = (bf16[128,1536]{1,0:T(8,128)(2,1)S(1)}, bf16[128,1536]{1,0:T(8,128)(2,1)S(1)}, u32[]{:S(2)}, u32[]{:S(2)}) collective-permute-start(bf16[128,1536]{1,0:T(8,128)(2,1)S(1)} %get-tuple-element.37), channel_id=1, source_target_pairs={{0,4},{2,6},{4,0},{6,2},{8,12},{10,14},{12,8},{14,10},{16,20},{18,... | collective-permute-start | bytes 1179656 | tf_op jit(solution)/shard_map/ppermute | solution.py:392
  223.7 40.9 %collective-permute-start.18 = (bf16[128,1536]{1,0:T(8,128)(2,1)}, bf16[128,1536]{1,0:T(8,128)(2,1)}, u32[]{:S(2)}, u32[]{:S(2)}) collective-permute-start(bf16[128,1536]{1,0:T(8,128)(2,1)} %get-tuple-element.47), channel_id=1, source_target_pairs={{0,2},{2,0},{4,6},{6,4},{8,10},{10,8},{12,14},{14,12},{16,18},{18,... | collective-permute-start | bytes 1179656 | tf_op jit(solution)/shard_map/ppermute | solution.py:392
  233.1 39.6 %collective-permute-start.28 = (bf16[128,1536]{1,0:T(8,128)(2,1)}, bf16[128,1536]{1,0:T(8,128)(2,1)S(1)}, u32[]{:S(2)}, u32[]{:S(2)}) collective-permute-start(bf16[128,1536]{1,0:T(8,128)(2,1)} %get-tuple-element.50), channel_id=1, source_target_pairs={{0,2},{2,0},{4,6},{6,4},{8,10},{10,8},{12,14},{14,12},{16,18},{18,... | collective-permute-start | bytes 1179656 | tf_op jit(solution)/shard_map/ppermute | solution.py:392
  234.4 38.4 %collective-permute-start.29 = (bf16[128,1536]{1,0:T(8,128)(2,1)}, bf16[128,1536]{1,0:T(8,128)(2,1)S(1)}, u32[]{:S(2)}, u32[]{:S(2)}) collective-permute-start(bf16[128,1536]{1,0:T(8,128)(2,1)} %get-tuple-element.51), channel_id=1, source_target_pairs={{0,4},{2,6},{4,0},{6,2},{8,12},{10,14},{12,8},{14,10},{16,20},{18,... | collective-permute-start | bytes 1179656 | tf_op jit(solution)/shard_map/ppermute | solution.py:392
  235.9 40.6 %collective-permute-start.39 = (bf16[128,1536]{1,0:T(8,128)(2,1)}, bf16[128,1536]{1,0:T(8,128)(2,1)S(1)}, u32[]{:S(2)}, u32[]{:S(2)}) collective-permute-start(bf16[128,1536]{1,0:T(8,128)(2,1)} %get-tuple-element.57), channel_id=1, source_target_pairs={{0,2},{2,0},{4,6},{6,4},{8,10},{10,8},{12,14},{14,12},{16,18},{18,... | collective-permute-start | bytes 1179656 | tf_op jit(solution)/shard_map/ppermute | solution.py:392
  238.2 38.3 %collective-permute-start.40 = (bf16[128,1536]{1,0:T(8,128)(2,1)}, bf16[128,1536]{1,0:T(8,128)(2,1)S(1)}, u32[]{:S(2)}, u32[]{:S(2)}) collective-permute-start(bf16[128,1536]{1,0:T(8,128)(2,1)} %get-tuple-element.58), channel_id=1, source_target_pairs={{0,4},{2,6},{4,0},{6,2},{8,12},{10,14},{12,8},{14,10},{16,20},{18,... | collective-permute-start | bytes 1179656 | tf_op jit(solution)/shard_map/ppermute | solution.py:392
  264.5 46.4 %collective-permute-start.7 = (bf16[128,1536]{1,0:T(8,128)(2,1)S(1)}, bf16[128,1536]{1,0:T(8,128)(2,1)S(1)}, u32[]{:S(2)}, u32[]{:S(2)}) collective-permute-start(bf16[128,1536]{1,0:T(8,128)(2,1)S(1)} %get-tuple-element.39), channel_id=1, source_target_pairs={{0,4},{2,6},{4,0},{6,2},{8,12},{10,14},{12,8},{14,10},{16,20},{18,... | collective-permute-start | bytes 1179656 | tf_op jit(solution)/shard_map/ppermute | solution.py:392
  287.6 23.3 %collective-permute-start.8 = (bf16[128,1536]{1,0:T(8,128)(2,1)S(1)}, bf16[128,1536]{1,0:T(8,128)(2,1)S(1)}, u32[]{:S(2)}, u32[]{:S(2)}) collective-permute-start(bf16[128,1536]{1,0:T(8,128)(2,1)S(1)} %get-tuple-element.40), channel_id=1, source_target_pairs={{0,2},{2,0},{4,6},{6,4},{8,10},{10,8},{12,14},{14,12},{16,18},{18,... | collective-permute-start | bytes 1179656 | tf_op jit(solution)/shard_map/ppermute | solution.py:392
  288.2 29.0 %collective-permute-start.19 = (bf16[128,3072]{1,0:T(8,128)(2,1)S(1)}, bf16[128,3072]{1,0:T(8,128)(2,1)S(1)}, u32[]{:S(2)}, u32[]{:S(2)}) collective-permute-start(bf16[128,3072]{1,0:T(8,128)(2,1)S(1)} %sum_1.1), channel_id=1, source_target_pairs={{0,8},{2,10},{4,12},{6,14},{8,0},{10,2},{12,4},{14,6},{16,24},{18,... | collective-permute-start | bytes 2359304 | tf_op jit(solution)/shard_map/ppermute | solution.py:392
  292.7 54.7 %collective-permute-start.32 = (bf16[128,3072]{1,0:T(8,128)(2,1)S(1)}, bf16[128,3072]{1,0:T(8,128)(2,1)S(1)}, u32[]{:S(2)}, u32[]{:S(2)}) collective-permute-start(bf16[128,3072]{1,0:T(8,128)(2,1)S(1)} %sum_2.1), channel_id=1, source_target_pairs={{0,16},{2,18},{4,20},{6,22},{8,24},{10,26},{12,28},{14,30},{16,0},... | collective-permute-start | bytes 2359304 | tf_op jit(solution)/shard_map/ppermute | solution.py:392
  296.7 65.4 %collective-permute-start.43 = (bf16[128,3072]{1,0:T(8,128)(2,1)S(1)}, bf16[128,3072]{1,0:T(8,128)(2,1)S(1)}, u32[]{:S(2)}, u32[]{:S(2)}) collective-permute-start(bf16[128,3072]{1,0:T(8,128)(2,1)S(1)} %sum_3.1), channel_id=1, source_target_pairs={{0,24},{2,26},{4,28},{6,30},{8,16},{10,18},{12,20},{14,22},{16,8},... | collective-permute-start | bytes 2359304 | tf_op jit(solution)/shard_map/ppermute | solution.py:392
  (81 other events, 734.8 us)
